TPU v7x, 32 devices: a whole 2x2x4 slice. The times are simulated.
32 devices in a mesh: seq: 16 (over z, y, core), mp: 2 (over x).
Axes of the slice: x: 2, y: 2, z: 4, core: 2. Of those that a mesh axis runs over, the one named last changes fastest.
Arguments:
- normed: bfloat16 [8192, 2048], P('seq', 'mp'), may hold values from -18 to 18
- router: bfloat16 [2048], replicated, may hold values from -0.125 to 0.125
- light_qkv: bfloat16 [3, 2048, 1024], P(None, None, 'mp'), may hold values from -0.125 to 0.125
- light_out: bfloat16 [1024, 2048], P('mp'), may hold values from -0.1875 to 0.1875
- heavy_qkv: bfloat16 [3, 2048, 1024], P(None, 'seq', 'mp'), may hold values from -0.125 to 0.125
- heavy_out: bfloat16 [1024, 2048], P('mp', 'seq'), may hold values from -0.1875 to 0.1875
- query_slots: int32 [16, 32], P('seq'), may hold values from 0 to 511, as said below
- query_count: int32 [16], P('seq'), may hold values from 1 to 32, 256 in all
- key_slots: int32 [16, 32], P('seq'), may hold values from 0 to 511, as said below
- key_count: int32 [16], P('seq'), may hold values from 1 to 32, 256 in all
Outputs:
- mixed: bfloat16 [8192, 2048], P('seq', 'mp')
Inputs may be any that keep to these rules, and one draw needn't show every extreme that they name: `query_slots`: each row holds 32 distinct positions of one shard's 512 tokens; only the first query_count entries of a row are live. `key_slots`: each row holds 32 distinct positions of one shard's 512 tokens; only the first key_count entries of a row are live. `query_count`: the counts sum to 256 and the largest is exactly 32. `key_count`: the counts sum to 256 and the largest is exactly 32.
All inputs are finite; a program needn't handle non-finite values.
Results may differ from a plain program's by a relative error of at most 0.012.
Values may be sent and summed in bfloat16 or wider, within the bound.
A program may use at most 128 MiB of HBM per device.

v0:
```python
import jax
import jax.numpy as jnp
from jax import lax
from jax.sharding import PartitionSpec as P

HEAD_DIM = 64
RADIUS = 64


NEG = -1e30


def padded(cells, sides, width):
    for axis, dim in sides:
        count = lax.axis_size(axis)
        ends = count - 1
        head = lax.slice_in_dim(cells, 0, width, axis=dim)
        tail = lax.slice_in_dim(cells, cells.shape[dim] - width, cells.shape[dim], axis=dim)
        cells = jnp.concatenate(
            [
                lax.ppermute(tail, axis, [(i, (i + 1) % count) for i in range(ends)]),
                cells,
                lax.ppermute(head, axis, [((i + 1) % count, i) for i in range(ends)]),
            ],
            axis=dim,
        )
    return cells


def mix_heads(queries, key_rows, value_rows, allowed):
    length = queries.shape[0]
    head_count = queries.shape[1] // HEAD_DIM
    query_heads = queries.reshape(length, head_count, HEAD_DIM)
    key_heads = key_rows.reshape(key_rows.shape[0], head_count, HEAD_DIM)
    value_heads = value_rows.reshape(value_rows.shape[0], head_count, HEAD_DIM)
    scores = jnp.einsum(
        "qhe,khe->hqk", query_heads, key_heads, preferred_element_type=jnp.float32
    ) * HEAD_DIM ** (-0.5)
    scores = jnp.where(allowed[None], scores, NEG)
    row_peak = jnp.max(scores, axis=2, keepdims=True)
    weights = jnp.where(allowed[None], jnp.exp(scores - row_peak), 0.0)
    row_total = jnp.sum(weights, axis=2)
    blended = jnp.einsum(
        "hqk,khe->qhe",
        weights.astype(jnp.bfloat16),
        value_heads,
        preferred_element_type=jnp.float32,
    )
    blended = blended / jnp.transpose(row_total)[:, :, None]
    return blended.reshape(length, head_count * HEAD_DIM).astype(jnp.bfloat16)


def shards(
    normed,
    router,
    light_qkv,
    light_out,
    heavy_qkv,
    heavy_out,
    query_slots,
    query_count,
    key_slots,
    key_count,
):
    local_rows = normed.shape[0]
    shard_index = lax.axis_index("seq")
    shard_total = lax.axis_size("seq")
    capacity = query_slots.shape[1]
    features = lax.all_gather(normed, "mp", axis=1, tiled=True)
    queries = jnp.dot(features, light_qkv[0], preferred_element_type=jnp.float32).astype(
        jnp.bfloat16
    )
    paired = jnp.einsum(
        "td,cdh->cth", features, light_qkv[1:], preferred_element_type=jnp.float32
    ).astype(jnp.bfloat16)
    paired = padded(paired, (("seq", 1),), RADIUS)
    key_rows = paired[0]
    value_rows = paired[1]
    block_rows = min(512, local_rows)
    first_row = shard_index * local_rows
    query_pos = first_row + 0 + jnp.arange(block_rows, dtype=jnp.int32)
    key_pos = first_row + 0 - RADIUS + jnp.arange(block_rows + 2 * RADIUS, dtype=jnp.int32)
    distance = jnp.abs(query_pos[:, None] - key_pos[None, :])
    allowed = (
        (distance <= RADIUS)
        & (key_pos[None, :] >= 0)
        & (key_pos[None, :] < local_rows * shard_total)
    )
    outputs = mix_heads(queries, key_rows, value_rows, allowed)
    light_part = jnp.dot(outputs, light_out, preferred_element_type=jnp.float32)
    slot_range = jnp.arange(capacity, dtype=jnp.int32)
    query_live = slot_range < query_count[0]
    key_live = (slot_range < key_count[0]).astype(jnp.bfloat16)
    query_inputs = features[query_slots[0]]
    key_inputs = features[key_slots[0]]
    portion = lax.all_gather(heavy_qkv, "seq", axis=1, tiled=True)
    heavy_query = jnp.dot(query_inputs, portion[0], preferred_element_type=jnp.float32)
    heavy_key = jnp.dot(key_inputs, portion[1], preferred_element_type=jnp.float32)
    heavy_value = jnp.dot(key_inputs, portion[2], preferred_element_type=jnp.float32)
    heavy_query = heavy_query.astype(jnp.bfloat16)
    heavy_key = heavy_key.astype(jnp.bfloat16)
    heavy_value = heavy_value.astype(jnp.bfloat16)
    head_count = heavy_query.shape[1] // HEAD_DIM
    scale = HEAD_DIM ** (-0.5)
    query_heads = heavy_query.reshape(capacity, head_count, HEAD_DIM)
    row_peak = jnp.full((capacity, head_count), NEG, jnp.float32)
    key_part = lax.all_gather(heavy_key, "seq", axis=0, tiled=True)
    value_part = lax.all_gather(heavy_value, "seq", axis=0, tiled=True)
    live_part = lax.all_gather(key_live, "seq", axis=0, tiled=True)
    length = key_part.shape[0]
    key_heads = key_part.reshape(length, head_count, HEAD_DIM)
    value_heads = value_part.reshape(length, head_count, HEAD_DIM)
    live = live_part[None, None, :] > 0
    scores = (
        jnp.einsum("qhe,khe->qhk", query_heads, key_heads, preferred_element_type=jnp.float32)
        * scale
    )
    scores = jnp.where(live, scores, NEG)
    new_peak = jnp.maximum(row_peak, jnp.max(scores, axis=2))
    weights = jnp.where(live, jnp.exp(scores - new_peak[:, :, None]), 0.0)
    row_total = jnp.sum(weights, axis=2)
    blended = jnp.einsum(
        "qhk,khe->qhe",
        weights.astype(jnp.bfloat16),
        value_heads,
        preferred_element_type=jnp.float32,
    )
    row_peak, row_total, blended = (new_peak, row_total, blended)
    blended = blended / row_total[:, :, None]
    heavy_context = blended.reshape(capacity, head_count * HEAD_DIM).astype(jnp.bfloat16)
    gate = jax.nn.sigmoid(jnp.dot(query_inputs, router, preferred_element_type=jnp.float32))
    gate = jnp.where(query_live, gate, 0.0)
    heavy_rows = (
        jnp.dot(
            heavy_context,
            lax.all_gather(heavy_out, "seq", axis=1, tiled=True),
            preferred_element_type=jnp.float32,
        )
        * gate[:, None]
    )
    combined = light_part.at[query_slots[0]].add(heavy_rows)
    return lax.psum_scatter(combined, "mp", scatter_dimension=1, tiled=True).astype(jnp.bfloat16)


def solution(mesh):
    in_specs = (
        P("seq", "mp"),
        P(),
        P(None, None, "mp"),
        P("mp", None),
        P(None, "seq", "mp"),
        P("mp", "seq"),
        P("seq", None),
        P("seq"),
        P("seq", None),
        P("seq"),
    )
    out_specs = P("seq", "mp")
    return jax.shard_map(shards, mesh=mesh, in_specs=in_specs, out_specs=out_specs, check_vma=False)
```

profile of v0, /device:TPU:0, one launch (start us, length us, event | category | flops | bytes accessed | tf_op | source)
XLA Modules:
  0.0 228.4 jit_solution(15369992581384270103)
XLA Ops:
  10.8 1.2 dynamic-slice
  13.0 34.9 %all-reduce = bf16[512]{0:T(512)(128)(2,1)S(1)} all-reduce(bf16[512]{0:T(512)(128)(2,1)S(1)} %dynamic-update-slice), channel_id=1, replica_groups=mesh['seq'=16,'mp'=2] {'seq'}, use_global_device_ids=true, to_apply=%add | all-reduce | flops 512 | bytes 2048
  49.3 1.2 fusion.33
  50.5 5.3 %fusion.21 = bf16[2,512,512]{2,1,0:T(8,128)(2,1)S(1)} fusion(bf16[3,2048,512]{2,1,0:T(8,128)(2,1)} %param.12, bf16[512,2048]{1,0:T(8,128)(2,1)} %all-gather.4.cloned.1.call-done), kind=kOutput, calls=%fused_computation.26 | convolution fusion | flops 2148007936 | bytes 7340032 | tf_op jit(solution)/shard_map/td,cdh->cth/dot_general | solution.py:73
  56.5 1.3 collective-permute-start
  57.8 1.5 collective-permute-start.1
  59.3 3.7 %fusion.34 = bf16[512,512]{0,1:T(8,128)(2,1)} fusion(bf16[512,2048]{1,0:T(8,128)(2,1)S(1)} %copy-done.1, bf16[3,2048,512]{2,1,0:T(8,128)(2,1)} %param.12), kind=kOutput, calls=%fused_computation.33 | convolution fusion | flops 1074003968 | bytes 4718592 | tf_op jit(solution)/shard_map/dot_general | solution.py:70
  63.0 2.6 %gather_fusion.1 = bf16[32,2048]{1,0:T(8,128)(2,1)S(1)} fusion(bf16[512,2048]{1,0:T(8,128)(2,1)} %all-gather.4.cloned.1.call-done, s32[1024]{0:T(1024)S(1)} %pad_clamp_fusion), kind=kCustom, calls=%fused_computation.1 | custom fusion | bytes 262272 | tf_op jit(solution)/shard_map/gather | solution.py:94
  65.7 2.7 %gather_fusion = bf16[32,2048]{1,0:T(8,128)(2,1)S(1)} fusion(bf16[512,2048]{1,0:T(8,128)(2,1)} %all-gather.4.cloned.1.call-done, s32[1024]{0:T(1024)S(1)} %pad_clamp_fusion.1), kind=kCustom, calls=%fused_computation | custom fusion | bytes 262272 | tf_op jit(solution)/shard_map/gather | solution.py:95
  69.6 1.1 copy.17
  71.0 8.4 %fusion.70 = (f32[8,512]{1,0:T(8,128)S(1)}, bf16[8,512,640]{2,1,0:T(8,128)(2,1)}) fusion(pred[512,640]{1,0:T(8,128)(4,1)} %fusion.33, bf16[512,8,64]{0,2,1:T(8,128)(2,1)} %bitcast.98, bf16[640,8,64]{0,2,1:T(8,128)(2,1)} %bitcast.94), kind=kOutput, calls=%fused_computation.76 | convolution fusion | flops 351273600 | bytes 6766592 | tf_op jit(solution)/shard_map/sub | solution.py:41
  79.4 4.2 %fusion.37 = bf16[512,8,64]{0,2,1:T(8,128)(2,1)S(1)} fusion(bf16[640,8,64]{0,2,1:T(8,128)(2,1)S(1)} %bitcast.95, bf16[8,512,640]{2,1,0:T(8,128)(2,1)} %get-tuple-element.10, f32[512,8]{0,1:T(8,128)S(1)} %bitcast.99), kind=kOutput, calls=%fused_computation.34 | convolution fusion | flops 336068608 | bytes 6438912 | tf_op jit(solution)/shard_map/hqk,khe->qhe/dot_general | solution.py:43
  83.7 3.3 %fusion.72 = f32[512,2048]{1,0:T(8,128)} fusion(bf16[512,512]{0,1:T(8,128)(2,1)S(1)} %bitcast.97, bf16[512,2048]{1,0:T(8,128)(2,1)S(1)} %copy-done), kind=kOutput, calls=%fused_computation.78 | convolution fusion | flops 1073741824 | bytes 6815744 | tf_op jit(solution)/shard_map/dot_general | solution.py:90
  86.9 22.2 %all-gather.6.cloned.1.call-done = bf16[3,2048,512]{2,1,0:T(8,128)(2,1)} async-done(((bf16[3,128,512]{2,1,0:T(8,128)(2,1)}), bf16[3,2048,512]{2,1,0:T(8,128)(2,1)}) %all-gather.6.cloned.1.call-update) | async-done | bytes 6291472 | tf_op jit(solution)/shard_map/all_gather | solution.py:96
  109.2 2.0 fusion.47
  111.3 2.0 fusion.48
  113.4 20.8 %all_gather.22 = bf16[512,512]{1,0:T(8,128)(2,1)S(1)} all-gather(bf16[32,512]{1,0:T(8,128)(2,1)S(1)} %fusion.48), channel_id=1, replica_groups=mesh['seq'=16,'mp'=2] {'seq'}, dimensions={0}, use_global_device_ids=true | all-gather | bytes 557056 | tf_op jit(solution)/shard_map/all_gather | solution.py:107
  134.4 2.0 fusion.46
  136.4 20.5 %all_gather.20 = bf16[512,512]{1,0:T(8,128)(2,1)S(1)} all-gather(bf16[32,512]{1,0:T(8,128)(2,1)S(1)} %fusion.46), channel_id=1, replica_groups=mesh['seq'=16,'mp'=2] {'seq'}, dimensions={0}, use_global_device_ids=true | all-gather | bytes 557056 | tf_op jit(solution)/shard_map/all_gather | solution.py:108
  158.5 1.4 fusion.45
  160.1 2.1 convolution_multiply_fusion
  162.1 5.1 %scatter_fusion = f32[512,2048]{1,0:T(8,128)} fusion(f32[512,2048]{1,0:T(8,128)} %fusion.72, s32[32]{0:T(128)S(1)} %copy-done.5, f32[32,2048]{1,0:T(8,128)S(1)} %convolution_multiply_fusion), kind=kCustom, calls=%fused_computation.2 | custom fusion | flops 65536 | bytes 786560 | tf_op jit(solution)/shard_map/scatter-add | solution.py:141
  167.3 51.9 %reduce-scatter.2.cloned.1.call-done = f32[512,1024]{1,0:T(8,128)} async-done(((f32[512,2048]{1,0:T(8,128)}), f32[512,1024]{1,0:T(8,128)}) %reduce-scatter.2.cloned.1.call-update) | async-done | bytes 2097168 | tf_op jit(solution)/shard_map/reduce_scatter | solution.py:142
  219.2 2.7 %convert_element_type.55 = bf16[512,1024]{1,0:T(8,128)(2,1)} convert(f32[512,1024]{1,0:T(8,128)} %reduce-scatter.2.cloned.1.call-done) | non-fusion elementwise | flops 524288 | bytes 3145728 | tf_op jit(solution)/shard_map/convert_element_type | solution.py:142
  (49 shorter events, 8.8 us)
Async XLA Ops:
  6.5 77.1 %copy-start = (bf16[512,2048]{1,0:T(8,128)(2,1)S(1)}, bf16[512,2048]{1,0:T(8,128)(2,1)}, u32[]{:S(2)}) copy-start(bf16[512,2048]{1,0:T(8,128)(2,1)} %param.13) | copy-start | bytes 6291460
  6.5 44.0 %all-gather.4.cloned.1.call-start = ((), (), s32[]{:S(2)}) async-start(), calls=%async_computation.1 | async-start | bytes 3145728 | tf_op jit(solution)/shard_map/all_gather | solution.py:69
  7.3 101.9 %all-gather.6.cloned.1.call-start = ((), (), s32[]{:S(2)}) async-start(), calls=%async_computation.2 | async-start | bytes 6684672 | tf_op jit(solution)/shard_map/all_gather | solution.py:96
  8.0 152.0 %all-gather.8.cloned.1.call-start = ((), (), s32[]{:S(2)}) async-start(), calls=%async_computation.3 | async-start | bytes 2228224 | tf_op jit(solution)/shard_map/all_gather | solution.py:136
  8.7 210.4 %reduce-scatter.2.cloned.1.call-start = ((), (), s32[]{:S(2)}) async-start(), calls=%async_computation.4 | async-start | bytes 6291456 | tf_op jit(solution)/shard_map/reduce_scatter | solution.py:142
  9.5 41.0 %copy-start.4 = (s32[32]{0:T(128)}, s32[32]{0:T(128)S(1)}, u32[]{:S(2)}) copy-start(s32[32]{0:T(128)S(1)} %fusion.63) | copy-start | bytes 388
  50.5 8.8 %copy-start.1 = (bf16[512,2048]{1,0:T(8,128)(2,1)S(1)}, bf16[512,2048]{1,0:T(8,128)(2,1)}, u32[]{:S(2)}) copy-start(bf16[512,2048]{1,0:T(8,128)(2,1)} %all-gather.4.cloned.1.call-done) | copy-start | bytes 6291460
  56.5 12.0 %collective-permute-start = (bf16[2,64,512]{2,1,0:T(8,128)(2,1)}, bf16[2,64,512]{2,1,0:T(8,128)(2,1)S(1)}, u32[]{:S(2)}, u32[]{:S(2)}) collective-permute-start(bf16[2,64,512]{2,1,0:T(8,128)(2,1)} %get-tuple-element.7), channel_id=1, source_target_pairs={{0,2},{2,4},{4,6},{6,8},{8,10},{10,12},{12,14},{14,16},{16,18},{18... | collective-permute-start | bytes 393224 | tf_op jit(solution)/shard_map/ppermute | solution.py:21
  57.8 10.7 %collective-permute-start.1 = (bf16[2,64,512]{2,1,0:T(8,128)(2,1)}, bf16[2,64,512]{2,1,0:T(8,128)(2,1)}, u32[]{:S(2)}, u32[]{:S(2)}) collective-permute-start(bf16[2,64,512]{2,1,0:T(8,128)(2,1)} %get-tuple-element.8), channel_id=1, source_target_pairs={{2,0},{4,2},{6,4},{8,6},{10,8},{12,10},{14,12},{16,14},{18,16},{20... | collective-permute-start | bytes 393224 | tf_op jit(solution)/shard_map/ppermute | solution.py:23
  65.6 2.9 %copy-start.2 = (bf16[32,2048]{1,0:T(8,128)(2,1)}, bf16[32,2048]{1,0:T(8,128)(2,1)S(1)}, u32[]{:S(2)}) copy-start(bf16[32,2048]{1,0:T(8,128)(2,1)S(1)} %gather_fusion.1) | copy-start | bytes 393220
  83.7 25.5 %copy-start.3 = (bf16[32,2048]{1,0:T(8,128)(2,1)S(1)}, bf16[32,2048]{1,0:T(8,128)(2,1)}, u32[]{:S(2)}) copy-start(bf16[32,2048]{1,0:T(8,128)(2,1)} %copy-done.2) | copy-start | bytes 393220
  158.2 3.9 %copy-start.5 = (s32[32]{0:T(128)S(1)}, s32[32]{0:T(128)}, u32[]{:S(2)}) copy-start(s32[32]{0:T(128)} %copy-done.4) | copy-start | bytes 388
Sparse Core Ops, SparseCore 0:
  8.9 35.8 all-gather.3
  46.9 62.1 all-gather.5
  111.3 43.2 all-gather.7
  167.4 51.7 reduce-scatter.1
where the time goes:
time: 229 us; the launch traced here: 228 us
  blocking collectives  76.3 us (33%)
  waiting for transfers between devices  76.2 us (33%)
  matrix products  34.9 us (15%)
  between operations  15.3 us (7%)
  other arithmetic  11.7 us (5%)
  local copies, waits for them, and re-layouts  11.2 us (5%)
  starting transfers between devices  2.87 us (1%)
    reduce_scatter x1, waiting for transfers between devices, shards(): lax.psum_scatter(combined, 'mp', scatter_dimension=1, tiled=True)  51.9 us
    unnamed x1, blocking collectives  34.9 us
    all_gather x1, waiting for transfers between devices, shards(): portion = lax.all_gather(heavy_qkv, 'seq', axis=1, tiled=True)  22.2 us
    all_gather x1, blocking collectives, shards(): key_part = lax.all_gather(heavy_key, 'seq', axis=0, tiled=True)  20.8 us
    all_gather x1, blocking collectives, shards(): value_part = lax.all_gather(heavy_value, 'seq', axis=0, tiled=True)  20.5 us
    sub x1, matrix products, mix_heads(): weights = jnp.where(allowed[None], jnp.exp(scores - row_peak), 0.0)  8.44 us
    dot_general x1, matrix products, shards(): jnp.einsum('td,cdh->cth', features, light_qkv[1:], preferred_element_type...  5.29 us
    scatter-add x1, other arithmetic, shards(): combined = light_part.at[query_slots[0]].add(heavy_rows)  5.12 us
  transfers between devices with their start and end apart: 6, of which 2 were waited for; matrix products, arithmetic and copies ran while one was open for 21% of the time, Pallas kernels for 0%

commit v1 on v0

--- a/solution.py
+++ b/solution.py
@@ -66,13 +66,19 @@
     shard_index = lax.axis_index("seq")
     shard_total = lax.axis_size("seq")
     capacity = query_slots.shape[1]
-    features = lax.all_gather(normed, "mp", axis=1, tiled=True)
-    queries = jnp.dot(features, light_qkv[0], preferred_element_type=jnp.float32).astype(
-        jnp.bfloat16
+    width = normed.shape[1]
+    me = lax.axis_index("mp")
+    swap = [(0, 1), (1, 0)]
+    other = lax.ppermute(normed, "mp", swap)
+    qkv_mine = lax.dynamic_slice_in_dim(light_qkv, me * width, width, axis=1)
+    qkv_other = lax.dynamic_slice_in_dim(light_qkv, (1 - me) * width, width, axis=1)
+    product = jnp.einsum("td,cdh->cth", normed, qkv_mine, preferred_element_type=jnp.float32)
+    product = product + jnp.einsum(
+        "td,cdh->cth", other, qkv_other, preferred_element_type=jnp.float32
     )
-    paired = jnp.einsum(
-        "td,cdh->cth", features, light_qkv[1:], preferred_element_type=jnp.float32
-    ).astype(jnp.bfloat16)
+    product = product.astype(jnp.bfloat16)
+    queries = product[0]
+    paired = product[1:]
     paired = padded(paired, (("seq", 1),), RADIUS)
     key_rows = paired[0]
     value_rows = paired[1]
@@ -87,12 +93,22 @@
         & (key_pos[None, :] < local_rows * shard_total)
     )
     outputs = mix_heads(queries, key_rows, value_rows, allowed)
-    light_part = jnp.dot(outputs, light_out, preferred_element_type=jnp.float32)
+    out_mine = lax.dynamic_slice_in_dim(light_out, me * width, width, axis=1)
+    out_other = lax.dynamic_slice_in_dim(light_out, (1 - me) * width, width, axis=1)
+    away = jnp.dot(outputs, out_other, preferred_element_type=jnp.float32).astype(jnp.bfloat16)
+    arrived = lax.ppermute(away, "mp", swap)
+    home = jnp.dot(outputs, out_mine, preferred_element_type=jnp.float32)
     slot_range = jnp.arange(capacity, dtype=jnp.int32)
     query_live = slot_range < query_count[0]
     key_live = (slot_range < key_count[0]).astype(jnp.bfloat16)
-    query_inputs = features[query_slots[0]]
-    key_inputs = features[key_slots[0]]
+    def rows_of(slots):
+        here, there = normed[slots], other[slots]
+        first = jnp.where(me == 0, here, there)
+        second = jnp.where(me == 0, there, here)
+        return jnp.concatenate([first, second], axis=1)
+
+    query_inputs = rows_of(query_slots[0])
+    key_inputs = rows_of(key_slots[0])
     portion = lax.all_gather(heavy_qkv, "seq", axis=1, tiled=True)
     heavy_query = jnp.dot(query_inputs, portion[0], preferred_element_type=jnp.float32)
     heavy_key = jnp.dot(key_inputs, portion[1], preferred_element_type=jnp.float32)
@@ -104,9 +120,13 @@
     scale = HEAD_DIM ** (-0.5)
     query_heads = heavy_query.reshape(capacity, head_count, HEAD_DIM)
     row_peak = jnp.full((capacity, head_count), NEG, jnp.float32)
-    key_part = lax.all_gather(heavy_key, "seq", axis=0, tiled=True)
-    value_part = lax.all_gather(heavy_value, "seq", axis=0, tiled=True)
-    live_part = lax.all_gather(key_live, "seq", axis=0, tiled=True)
+    size = heavy_key.shape[1]
+    marks = jnp.broadcast_to(key_live[:, None], (capacity, 128))
+    packed = jnp.concatenate([heavy_key, heavy_value, marks], axis=1)
+    packed = lax.all_gather(packed, "seq", axis=0, tiled=True)
+    key_part = packed[:, :size]
+    value_part = packed[:, size : 2 * size]
+    live_part = packed[:, 2 * size]
     length = key_part.shape[0]
     key_heads = key_part.reshape(length, head_count, HEAD_DIM)
     value_heads = value_part.reshape(length, head_count, HEAD_DIM)
@@ -138,8 +158,11 @@
         )
         * gate[:, None]
     )
-    combined = light_part.at[query_slots[0]].add(heavy_rows)
-    return lax.psum_scatter(combined, "mp", scatter_dimension=1, tiled=True).astype(jnp.bfloat16)
+    rows_mine = lax.dynamic_slice_in_dim(heavy_rows, me * width, width, axis=1)
+    rows_other = lax.dynamic_slice_in_dim(heavy_rows, (1 - me) * width, width, axis=1)
+    rows_mine = rows_mine + lax.ppermute(rows_other, "mp", swap)
+    combined = home + arrived.astype(jnp.float32)
+    return combined.at[query_slots[0]].add(rows_mine).astype(jnp.bfloat16)
 
 
 def solution(mesh):

time: 229 us -> 180 us (0.79)
  blocking collectives: 76.3 us -> 0 us
  waiting for transfers between devices: 76.2 us -> 87.6 us
  starting transfers between devices: 2.87 us -> 9.77 us
  local copies, waits for them, and re-layouts: 11.2 us -> 17.9 us
    reduce_scatter x1 -> x0, waiting for transfers between devices: 51.9 us -> none  [shards(): lax.psum_scatter(combined, 'mp', scatter_dimension=1, tiled=True)]
    all_gather x2 -> x0, blocking collectives: 41.3 us -> none  [the longest x1 20.8 us: shards(): key_part = lax.all_gather(heavy_key, 'seq', axis=0, tiled=True)]
    unnamed x1 -> x0, blocking collectives: 34.9 us -> none
    all_gather x1, waiting for transfers between devices: 0.02 us -> 28.1 us  [shards(): lax.all_gather(heavy_out, 'seq', axis=1, tiled=True)]
    ppermute x0 -> x3, waiting for transfers between devices: none -> 19.4 us  [the longest x1 17.3 us: shards(): other = lax.ppermute(normed, 'mp', swap)]
    all_gather x1, waiting for transfers between devices: 22.2 us -> 38.6 us  [shards(): portion = lax.all_gather(heavy_qkv, 'seq', axis=1, tiled=True)]
    slice x0 -> x6, local copies, waits for them, and re-layouts: none -> 9.3 us  [the longest x2 4.3 us: shards(): key_part = packed[:, :size]]
    ppermute x0 -> x3, starting transfers between devices: none -> 6.05 us  [the longest x1 3 us: shards(): other = lax.ppermute(normed, 'mp', swap)]
  transfers between devices with their start and end apart: 6 -> 8, of which waited for: 2 -> 4; matrix products, arithmetic and copies ran while one was open for 21% -> 31% of each run, Pallas kernels for 0% -> 0%
where the time goes in v1:
time: 180 us
  waiting for transfers between devices  87.6 us (49%)
  matrix products  36.9 us (20%)
  local copies, waits for them, and re-layouts  17.9 us (10%)
  between operations  14.7 us (8%)
  other arithmetic  12.7 us (7%)
  starting transfers between devices  9.77 us (5%)
    all_gather x1, waiting for transfers between devices, shards(): portion = lax.all_gather(heavy_qkv, 'seq', axis=1, tiled=True)  38.6 us
    all_gather x1, waiting for transfers between devices, shards(): lax.all_gather(heavy_out, 'seq', axis=1, tiled=True)  28.1 us
    ppermute x1, waiting for transfers between devices, shards(): other = lax.ppermute(normed, 'mp', swap)  17.3 us
    sub x1, matrix products, mix_heads(): weights = jnp.where(allowed[None], jnp.exp(scores - row_peak), 0.0)  8.43 us
    gather x4, local copies, waits for them, and re-layouts, rows_of(): here, there = (normed[slots], other[slots])  5.32 us
    slice x2, local copies, waits for them, and re-layouts, shards(): key_part = packed[:, :size]  4.3 us
    dot_general x1, matrix products, mix_heads(): jnp.einsum('hqk,khe->qhe', weights.astype(jnp.bfloat16), value_heads, pre...  4.2 us
    dot_general x1, matrix products, shards(): jnp.einsum('td,cdh->cth', normed, qkv_mine, preferred_element_type=jnp.fl...  3.77 us
  transfers between devices with their start and end apart: 8, of which 4 were waited for; matrix products, arithmetic and copies ran while one was open for 31% of the time, Pallas kernels for 0%

profile of v1, /device:TPU:0, one launch (start us, length us, event | category | flops | bytes accessed | tf_op | source)
XLA Modules:
  0.0 179.5 jit_solution(10494857819983072289)
XLA Ops:
  7.3 3.0 %collective-permute-start = (bf16[512,1024]{1,0:T(8,128)(2,1)}, bf16[512,1024]{1,0:T(8,128)(2,1)S(1)}, u32[]{:S(2)}, u32[]{:S(2)}) collective-permute-start(bf16[512,1024]{1,0:T(8,128)(2,1)} %param.10), channel_id=1, source_target_pairs={{0,1},{1,0},{2,3},{3,2},{4,5},{5,4},{6,7},{7,6},{8,9},{9,8},{10,11... | collective-permute-start | bytes 3145736 | tf_op jit(solution)/shard_map/ppermute | solution.py:72
  11.0 2.0 %gather_fusion.2 = bf16[32,1024]{1,0:T(8,128)(2,1)S(1)} fusion(bf16[512,1024]{1,0:T(8,128)(2,1)} %param.10, s32[1024]{0:T(1024)S(1)} %pad_clamp_fusion), kind=kCustom, calls=%fused_computation.2 | custom fusion | bytes 131200 | tf_op jit(solution)/shard_map/gather | solution.py:105
  13.7 2.0 %gather_fusion = bf16[32,1024]{1,0:T(8,128)(2,1)S(1)} fusion(bf16[512,1024]{1,0:T(8,128)(2,1)} %param.10, s32[1024]{0:T(1024)S(1)} %pad_clamp_fusion.1), kind=kCustom, calls=%fused_computation | custom fusion | bytes 131200 | tf_op jit(solution)/shard_map/gather | solution.py:105
  16.4 17.3 %collective-permute-done = bf16[512,1024]{1,0:T(8,128)(2,1)S(1)} collective-permute-done((bf16[512,1024]{1,0:T(8,128)(2,1)}, bf16[512,1024]{1,0:T(8,128)(2,1)S(1)}, u32[]{:S(2)}, u32[]{:S(2)}) %collective-permute-start) | collective-permute-done | bytes 1048608 | tf_op jit(solution)/shard_map/ppermute | solution.py:72
  35.6 38.6 %all-gather.4.cloned.1.call-done = bf16[3,2048,512]{2,1,0:T(8,128)(2,1)} async-done(((bf16[3,128,512]{2,1,0:T(8,128)(2,1)}), bf16[3,2048,512]{2,1,0:T(8,128)(2,1)}) %all-gather.4.cloned.1.call-update) | async-done | bytes 6291472 | tf_op jit(solution)/shard_map/all_gather | solution.py:112
  74.2 2.1 %fusion.34 = bf16[32,512]{1,0:T(8,128)(2,1)S(1)} fusion(bf16[3,2048,512]{2,1,0:T(8,128)(2,1)} %all-gather.4.cloned.1.call-done, bf16[32,1024]{1,0:T(8,128)(2,1)S(1)} %get-tuple-element.21, bf16[32,1024]{1,0:T(8,128)(2,1)S(1)} %get-tuple-element.22), kind=kOutput, calls=%fused_computation.43 | convolution fusion | flops 67387392 | bytes 2260992 | tf_op jit(solution)/shard_map/dot_general | solution.py:114
  76.4 2.1 %fusion.35 = bf16[32,512]{1,0:T(8,128)(2,1)S(1)} fusion(bf16[3,2048,512]{2,1,0:T(8,128)(2,1)} %all-gather.4.cloned.1.call-done, bf16[32,1024]{1,0:T(8,128)(2,1)S(1)} %get-tuple-element.21, bf16[32,1024]{1,0:T(8,128)(2,1)S(1)} %get-tuple-element.22), kind=kOutput, calls=%fused_computation.44 | convolution fusion | flops 67387392 | bytes 2260992 | tf_op jit(solution)/shard_map/dot_general | solution.py:115
  80.7 3.8 %fusion.9 = f32[3,512,512]{1,2,0:T(8,128)S(1)} fusion(bf16[3,2048,512]{2,1,0:T(8,128)(2,1)} %param.12, s32[]{:T(128)S(6)} %select_n.74, bf16[512,1024]{1,0:T(8,128)(2,1)S(1)} %copy-done.3), kind=kOutput, calls=%fused_computation.17 | convolution fusion | flops 1610612736 | bytes 7340036 | tf_op jit(solution)/shard_map/td,cdh->cth/dot_general | solution.py:75
  85.6 3.7 %fusion.14 = bf16[3,512,512]{2,1,0:T(8,128)(2,1)S(1)} fusion(f32[3,512,512]{1,2,0:T(8,128)S(1)} %fusion.9, bf16[3,2048,512]{2,1,0:T(8,128)(2,1)} %param.12, s32[]{:T(128)S(6)} %select_n.75, bf16[512,1024]{1,0:T(8,128)(2,1)S(1)} %copy-done.5), kind=kOutput, calls=%fused_computation.27 | convolution fusion | flops 1612185600 | bytes 8912900 | tf_op jit(solution)/shard_map/td,cdh->cth/dot_general | solution.py:76
  91.0 2.2 %collective-permute-start.1 = (bf16[2,64,512]{2,1,0:T(8,128)(2,1)}, bf16[2,64,512]{2,1,0:T(8,128)(2,1)S(1)}, u32[]{:S(2)}, u32[]{:S(2)}) collective-permute-start(bf16[2,64,512]{2,1,0:T(8,128)(2,1)} %get-tuple-element.5), channel_id=1, source_target_pairs={{0,2},{2,4},{4,6},{6,8},{8,10},{10,12},{12,14},{14,16},{16,18},{18... | collective-permute-start | bytes 393224 | tf_op jit(solution)/shard_map/ppermute | solution.py:21
  94.6 2.1 %copy.18 = bf16[1,512,512]{1,2,0:T(8,128)(2,1)} copy(bf16[1,512,512]{2,1,0:T(8,128)(2,1)} %slice.62) | data formatting | bytes 1048576 | tf_op jit(solution)/shard_map/slice | solution.py:80
  99.3 8.4 %fusion.77 = (f32[8,512]{1,0:T(8,128)S(1)}, bf16[8,512,640]{2,1,0:T(8,128)(2,1)}) fusion(pred[512,640]{1,0:T(8,128)(4,1)} %fusion.24, bf16[512,8,64]{0,2,1:T(8,128)(2,1)} %bitcast.86, bf16[640,8,64]{0,2,1:T(8,128)(2,1)} %bitcast.84), kind=kOutput, calls=%fused_computation.102 | convolution fusion | flops 351273600 | bytes 6766592 | tf_op jit(solution)/shard_map/sub | solution.py:41
  107.7 4.2 %fusion.25 = bf16[512,8,64]{0,2,1:T(8,128)(2,1)S(1)} fusion(bf16[640,8,64]{0,2,1:T(8,128)(2,1)S(1)} %bitcast.85, bf16[8,512,640]{2,1,0:T(8,128)(2,1)} %get-tuple-element.16, f32[512,8]{0,1:T(8,128)S(1)} %bitcast.88), kind=kOutput, calls=%fused_computation.35 | convolution fusion | flops 336068608 | bytes 6438912 | tf_op jit(solution)/shard_map/hqk,khe->qhe/dot_general | solution.py:43
  115.9 2.0 %fusion.36 = bf16[32,512]{1,0:T(8,128)(2,1)S(1)} fusion(bf16[3,2048,512]{2,1,0:T(8,128)(2,1)} %all-gather.4.cloned.1.call-done, bf16[32,1024]{1,0:T(8,128)(2,1)S(1)} %copy-done.7, bf16[32,1024]{1,0:T(8,128)(2,1)S(1)} %copy-done.6), kind=kOutput, calls=%fused_computation.45 | convolution fusion | flops 67387392 | bytes 2260992 | tf_op jit(solution)/shard_map/dot_general | solution.py:113
  118.1 2.3 %fusion.76 = (bf16[512,512]{1,0:T(8,128)(2,1)}, bf16[512,512]{1,0:T(8,128)(2,1)}) fusion(bf16[512,1152]{1,0:T(8,128)(2,1)} %all-gather.6.cloned.1.call-done), kind=kLoop, calls=%fused_computation.101 | loop fusion | bytes 2097152 | tf_op jit(solution)/shard_map/slice | solution.py:127
  120.3 2.0 %copy.21 = bf16[512,512]{0,1:T(8,128)(2,1)} copy(bf16[512,512]{1,0:T(8,128)(2,1)} %get-tuple-element.9) | data formatting | bytes 1048576 | tf_op jit(solution)/shard_map/slice | solution.py:127
  123.4 2.1 %fusion.78 = (f32[32,8]{0,1:T(8,128)S(1)}, f32[32,8,512]{2,0,1:T(8,128)}) fusion(bf16[512,8,64]{0,2,1:T(8,128)(2,1)} %bitcast.81, bf16[32,8,64]{2,1,0:T(8,128)(2,1)S(1)} %reshape.167, pred[512]{0:T(512)(128)(4,1)S(1)} %compare_reduce_fusion), kind=kOutput, calls=%fused_computation.103 | convolution fusion | flops 17170176 | bytes 1082880 | tf_op jit(solution)/shard_map/qhe,khe->qhk/dot_general | solution.py:135
  125.5 2.1 %copy.20 = bf16[512,512]{0,1:T(8,128)(2,1)} copy(bf16[512,512]{1,0:T(8,128)(2,1)} %get-tuple-element.10) | data formatting | bytes 1048576 | tf_op jit(solution)/shard_map/slice | solution.py:128
  130.6 28.1 %all-gather.8.cloned.1.call-done = bf16[512,2048]{1,0:T(8,128)(2,1)} async-done(((bf16[512,128]{1,0:T(8,128)(2,1)}), bf16[512,2048]{1,0:T(8,128)(2,1)}) %all-gather.8.cloned.1.call-update) | async-done | bytes 2097168 | tf_op jit(solution)/shard_map/all_gather | solution.py:156
  158.7 2.1 %convolution_multiply_fusion = f32[32,2048]{1,0:T(8,128)S(1)} fusion(bf16[32,512]{1,0:T(8,128)(2,1)S(1)} %convert_element_type.62, bf16[512,2048]{1,0:T(8,128)(2,1)} %all-gather.8.cloned.1.call-done, f32[32]{0:T(128)S(1)} %fusion.41), kind=kOutput, calls=%fused_computation.19 | convolution fusion | flops 67174400 | bytes 2392192 | tf_op jit(solution)/shard_map/dot_general | solution.py:154
  162.4 2.1 %convert_add_fusion = f32[512,1024]{1,0:T(8,128)} fusion(bf16[512,1024]{1,0:T(8,128)(2,1)S(1)} %collective-permute-done.3, bf16[512,512]{0,1:T(8,128)(2,1)S(1)} %bitcast.83, bf16[512,2048]{1,0:T(8,128)(2,1)S(1)} %copy-done, s32[]{:T(128)S(6)} %select_n.74), kind=kOutput, calls=%fused_computation.26 | convolution fusion | flops 537919488 | bytes 4718596 | tf_op jit(solution)/shard_map/dot_general | solution.py:100
  164.5 2.1 %collective-permute-done.4 = f32[32,1024]{1,0:T(8,128)S(1)} collective-permute-done((f32[32,1024]{1,0:T(8,128)S(1)}, f32[32,1024]{1,0:T(8,128)S(1)}, u32[]{:S(2)}, u32[]{:S(2)}) %collective-permute-start.4) | collective-permute-done | bytes 131104 | tf_op jit(solution)/shard_map/ppermute | solution.py:163
  166.6 3.7 %scatter_custom_fusion = f32[512,1024]{1,0:T(8,128)} fusion(f32[512,1024]{1,0:T(8,128)} %convert_add_fusion, s32[32]{0:T(128)S(1)} %fusion.65, f32[32,1024]{1,0:T(8,128)S(1)} %collective-permute-done.4, f32[32,2048]{1,0:T(8,128)S(1)} %convolution_multiply_fusion, s32[]{:T(128)} %constant.16.clone.1, s32[]{:T(128)S(6)} %select_n.74), kind=kCustom, calls=%fused_computation.66 | custom fusion | flops 65536 | bytes 2359812 | tf_op jit(solution)/shard_map/scatter-add | solution.py:165
  170.3 2.7 %convert_element_type.63 = bf16[512,1024]{1,0:T(8,128)(2,1)} convert(f32[512,1024]{1,0:T(8,128)} %scatter_custom_fusion) | non-fusion elementwise | flops 524288 | bytes 3145728 | tf_op jit(solution)/shard_map/convert_element_type | solution.py:165
  (63 shorter events, 22.0 us)
Async XLA Ops:
  6.5 106.2 %copy-start = (bf16[512,2048]{1,0:T(8,128)(2,1)S(1)}, bf16[512,2048]{1,0:T(8,128)(2,1)}, u32[]{:S(2)}) copy-start(bf16[512,2048]{1,0:T(8,128)(2,1)} %param.13) | copy-start | bytes 6291460
  6.5 67.7 %all-gather.4.cloned.1.call-start = ((), (), s32[]{:S(2)}) async-start(), calls=%async_computation | async-start | bytes 6684672 | tf_op jit(solution)/shard_map/all_gather | solution.py:112
  7.3 110.8 %all-gather.6.cloned.1.call-start = ((), (), s32[]{:S(2)}) async-start(), calls=%async_computation.1 | async-start | bytes 1253376 | tf_op jit(solution)/shard_map/all_gather | solution.py:126
  7.3 26.4 %collective-permute-start = (bf16[512,1024]{1,0:T(8,128)(2,1)}, bf16[512,1024]{1,0:T(8,128)(2,1)S(1)}, u32[]{:S(2)}, u32[]{:S(2)}) collective-permute-start(bf16[512,1024]{1,0:T(8,128)(2,1)} %param.10), channel_id=1, source_target_pairs={{0,1},{1,0},{2,3},{3,2},{4,5},{5,4},{6,7},{7,6},{8,9},{9,8},{10,11... | collective-permute-start | bytes 3145736 | tf_op jit(solution)/shard_map/ppermute | solution.py:72
  33.7 40.5 %copy-start.4 = (bf16[512,1024]{1,0:T(8,128)(2,1)}, bf16[512,1024]{1,0:T(8,128)(2,1)S(1)}, u32[]{:S(2)}) copy-start(bf16[512,1024]{1,0:T(8,128)(2,1)S(1)} %collective-permute-done) | copy-start | bytes 3145732
  74.2 5.7 %copy-start.8 = (bf16[2048]{0:T(1024)(128)(2,1)S(1)}, bf16[2048]{0:T(1024)(128)(2,1)}, u32[]{:S(2)}) copy-start(bf16[2048]{0:T(1024)(128)(2,1)} %param.11) | copy-start | bytes 12292
  74.2 6.4 %copy-start.3 = (bf16[512,1024]{1,0:T(8,128)(2,1)S(1)}, bf16[512,1024]{1,0:T(8,128)(2,1)}, u32[]{:S(2)}) copy-start(bf16[512,1024]{1,0:T(8,128)(2,1)} %param.10) | copy-start | bytes 3145732
  79.2 79.5 %all-gather.8.cloned.1.call-start = ((), (), s32[]{:S(2)}) async-start(), calls=%async_computation.2 | async-start | bytes 2228224 | tf_op jit(solution)/shard_map/all_gather | solution.py:156
  80.6 5.0 %copy-start.5 = (bf16[512,1024]{1,0:T(8,128)(2,1)S(1)}, bf16[512,1024]{1,0:T(8,128)(2,1)}, u32[]{:S(2)}) copy-start(bf16[512,1024]{1,0:T(8,128)(2,1)} %copy-done.4) | copy-start | bytes 3145732
  91.0 6.7 %collective-permute-start.1 = (bf16[2,64,512]{2,1,0:T(8,128)(2,1)}, bf16[2,64,512]{2,1,0:T(8,128)(2,1)S(1)}, u32[]{:S(2)}, u32[]{:S(2)}) collective-permute-start(bf16[2,64,512]{2,1,0:T(8,128)(2,1)} %get-tuple-element.5), channel_id=1, source_target_pairs={{0,2},{2,4},{4,6},{6,8},{8,10},{10,12},{12,14},{14,16},{16,18},{18... | collective-permute-start | bytes 393224 | tf_op jit(solution)/shard_map/ppermute | solution.py:21
  93.1 4.6 %collective-permute-start.2 = (bf16[2,64,512]{2,1,0:T(8,128)(2,1)S(1)}, bf16[2,64,512]{2,1,0:T(8,128)(2,1)S(1)}, u32[]{:S(2)}, u32[]{:S(2)}) collective-permute-start(bf16[2,64,512]{2,1,0:T(8,128)(2,1)S(1)} %get-tuple-element.6), channel_id=1, source_target_pairs={{2,0},{4,2},{6,4},{8,6},{10,8},{12,10},{14,12},{16,14},{18,16},{20... | collective-permute-start | bytes 393224 | tf_op jit(solution)/shard_map/ppermute | solution.py:23
  111.9 0.8 copy-start.1
  111.9 4.0 %copy-start.6 = (bf16[32,1024]{1,0:T(8,128)(2,1)S(1)}, bf16[32,1024]{1,0:T(8,128)(2,1)}, u32[]{:S(2)}) copy-start(bf16[32,1024]{1,0:T(8,128)(2,1)} %get-tuple-element.11) | copy-start | bytes 196612
  111.9 4.0 %copy-start.7 = (bf16[32,1024]{1,0:T(8,128)(2,1)S(1)}, bf16[32,1024]{1,0:T(8,128)(2,1)}, u32[]{:S(2)}) copy-start(bf16[32,1024]{1,0:T(8,128)(2,1)} %get-tuple-element.12) | copy-start | bytes 196612
  114.4 48.0 %collective-permute-start.3 = (bf16[512,1024]{1,0:T(8,128)(2,1)}, bf16[512,1024]{1,0:T(8,128)(2,1)S(1)}, u32[]{:S(2)}, u32[]{:S(2)}) collective-permute-start(bf16[512,1024]{1,0:T(8,128)(2,1)} %convolution_convert_fusion), channel_id=1, source_target_pairs={{0,1},{1,0},{2,3},{3,2},{4,5},{5,4},{6,7},{7,6},{8,9},{9,8},{10,11... | collective-permute-start | bytes 3145736 | tf_op jit(solution)/shard_map/ppermute | solution.py:99
  158.7 3.7 %copy-start.2 = (bf16[512,8,64]{0,2,1:T(8,128)(2,1)S(1)}, bf16[512,8,64]{0,2,1:T(8,128)(2,1)}, u32[]{:S(2)}) copy-start(bf16[512,8,64]{0,2,1:T(8,128)(2,1)} %copy-done.1) | copy-start | bytes 1572868
  160.8 5.7 %collective-permute-start.4 = (f32[32,1024]{1,0:T(8,128)S(1)}, f32[32,1024]{1,0:T(8,128)S(1)}, u32[]{:S(2)}, u32[]{:S(2)}) collective-permute-start(f32[32,1024]{1,0:T(8,128)S(1)} %constant_dynamic-slice_fusion), channel_id=1, source_target_pairs={{0,1},{1,0},{2,3},{3,2},{4,5},{5,4},{6,7},{7,6},{8,9},{9,8},{10,11... | collective-permute-start | bytes 393224 | tf_op jit(solution)/shard_map/ppermute | solution.py:163
Sparse Core Ops, SparseCore 0:
  9.5 64.6 all-gather.3
  79.3 36.9 all-gather.5
  118.5 40.1 all-gather.7

commit v2 on v0

v2 whole, which is shorter than its diff:
```python
import functools

import jax
import jax.numpy as jnp
from jax import lax
from jax.experimental import pallas as pl
from jax.experimental.pallas import tpu as pltpu
from jax.sharding import PartitionSpec as P

HEAD_DIM = 64
RADIUS = 64
PAIR = 2 * HEAD_DIM
BLOCK = 128
NEG = -1e30
F32 = jnp.float32
BF16 = jnp.bfloat16
MESH = pl.DeviceIdType.MESH
NT = (((1,), (1,)), ((), ()))


def dot(a, b):
    return jnp.dot(a, b, preferred_element_type=F32)


def dot_nt(a, b):
    return lax.dot_general(a, b, NT, preferred_element_type=F32)


def attend(q, k, v, allowed, scale):
    rows = q.shape[0]
    low = lax.broadcasted_iota(jnp.int32, q.shape, 1) < HEAD_DIM
    zero = jnp.zeros_like(q)
    both = jnp.concatenate([jnp.where(low, q, zero), jnp.where(low, zero, q)], axis=0)
    scores = jnp.where(allowed, dot_nt(both, k) * scale, NEG)
    weights = jnp.exp(scores - jnp.max(scores, axis=1, keepdims=True))
    total = jnp.sum(weights, axis=1, keepdims=True)
    blended = dot(weights.astype(BF16), v) / total
    return jnp.where(low, blended[:rows], blended[rows:]).astype(BF16)


def kernel(
    count,
    normed,
    router,
    light_qkv,
    light_out,
    heavy,
    query_col,
    query_row,
    key_col,
    query_count,
    key_count,
    result,
    other,
    wide,
    narrow,
    pool,
    share,
    queries,
    window,
    context,
    away,
    arrived,
    inputs,
    heavy_kv,
    rows_away,
    rows_in,
    load_sem,
    recv_sem,
    up_sem,
    down_sem,
    cross_sem,
    core_sem,
    feat_send,
    feat_recv,
    halo_send,
    halo_recv,
    out_send,
    out_recv,
    row_send,
    row_recv,
):
    tokens, width = normed.shape
    size = narrow.shape[0]
    depth = heavy.shape[1]
    cap = key_col.shape[0]
    scale = HEAD_DIM ** (-0.5)
    me = lax.axis_index("seq")
    part = lax.axis_index("mp")
    peer = 1 - part
    levels = count // 4
    z = me // 4
    y = (me // 2) % 2
    c = me % 2
    left = lax.rem(me + count - 1, count)
    right = lax.rem(me + 1, count)
    top = z < levels - 1
    bottom = z > 0

    def slot(o, yy, cc):
        return (o * 2 + yy) * 2 + cc

    to_peer = {"mp": peer}
    to_up = {"seq": jnp.minimum(me + 4, count - 1)}
    to_down = {"seq": jnp.maximum(me - 4, 0)}
    to_cross = {"seq": slot(z, 1 - y, c)}
    to_core = {"seq": slot(z, y, 1 - c)}

    barrier = pltpu.get_barrier_semaphore()
    for dest in (to_peer, to_cross, to_core, {"seq": left}, {"seq": right}):
        pl.semaphore_signal(barrier, inc=1, device_id=dest, device_id_type=MESH)

    @pl.when(top)
    def _():
        pl.semaphore_signal(barrier, inc=1, device_id=to_up, device_id_type=MESH)

    @pl.when(bottom)
    def _():
        pl.semaphore_signal(barrier, inc=1, device_id=to_down, device_id_type=MESH)

    load_qkv = pltpu.make_async_copy(light_qkv, wide, load_sem.at[0])
    load_qkv.start()
    load_out = pltpu.make_async_copy(light_out, narrow, load_sem.at[1])
    load_out.start()
    pool[:, pl.ds(pl.multiple_of(me * depth, depth), depth), :] = heavy[...]

    pl.semaphore_wait(barrier, 5 + top.astype(jnp.int32) + bottom.astype(jnp.int32))

    def remote(src, dst, send, recv, dest):
        return pltpu.make_async_remote_copy(
            src_ref=src,
            dst_ref=dst,
            send_sem=send,
            recv_sem=recv,
            device_id=dest,
            device_id_type=MESH,
        )

    def view(chunk, s):
        if chunk < 2:
            rows = pl.ds(pl.multiple_of(s * depth, depth), depth)
            return pool.at[pl.ds(2 * chunk, 2), rows, :]
        return heavy_kv.at[pl.ds(pl.multiple_of(s * cap, cap), cap), :]

    def hop(chunk, s, send, dest):
        return remote(view(chunk, s), view(chunk, s), send, recv_sem.at[chunk, s], dest)

    def up(chunk, o):
        return hop(chunk, slot(o, y, c), up_sem.at[chunk, o], to_up)

    def down(chunk, o):
        return hop(chunk, slot(o, y, c), down_sem.at[chunk, o], to_down)

    def cross(chunk, o):
        return hop(chunk, slot(o, y, c), cross_sem.at[chunk, o], to_cross)

    def core(chunk, o, yy):
        return hop(chunk, slot(o, yy, c), core_sem.at[chunk, o * 2 + yy], to_core)

    def landed(chunk, s):
        hop(chunk, s, core_sem.at[chunk, 0], to_core).wait_recv()

    def own(chunk):
        @pl.when(top)
        def _():
            up(chunk, z).start()

        @pl.when(bottom)
        def _():
            down(chunk, z).start()

        cross(chunk, z).start()
        core(chunk, z, y).start()

    def along(chunk, d):
        @pl.when(z - d >= 0)
        def _():
            o = z - d
            landed(chunk, slot(o, y, c))

            @pl.when(top)
            def _():
                up(chunk, o).start()

            cross(chunk, o).start()
            core(chunk, o, y).start()

        @pl.when(z + d < levels)
        def _():
            o = z + d
            landed(chunk, slot(o, y, c))

            @pl.when(bottom)
            def _():
                down(chunk, o).start()

            cross(chunk, o).start()
            core(chunk, o, y).start()

    def across(chunk, d):
        @pl.when(z - d >= 0)
        def _():
            landed(chunk, slot(z - d, 1 - y, c))
            core(chunk, z - d, 1 - y).start()

        if d > 0:

            @pl.when(z + d < levels)
            def _():
                landed(chunk, slot(z + d, 1 - y, c))
                core(chunk, z + d, 1 - y).start()

    def events(chunk):
        for d in range(1, levels):
            yield functools.partial(along, chunk, d)
            yield functools.partial(across, chunk, d - 1)
        yield functools.partial(across, chunk, levels - 1)

    pending = [list(events(chunk)) for chunk in range(3)]

    def advance(chunk, steps=None):
        steps = len(pending[chunk]) if steps is None else min(steps, len(pending[chunk]))
        for _ in range(steps):
            pending[chunk].pop(0)()

    def gathered(chunk):
        for o in range(levels):
            for yy in range(2):
                landed(chunk, slot(o, yy, 1 - c))

    def drain(chunk):
        for o in range(levels):

            @pl.when(top & (z >= o))
            def _():
                up(chunk, o).wait_send()

            @pl.when(bottom & (z <= o))
            def _():
                down(chunk, o).wait_send()

            cross(chunk, o).wait_send()
            for yy in range(2):
                core(chunk, o, yy).wait_send()

    half = tokens // 2

    def feature(i):
        rows = pl.ds(i * half, half)
        return remote(normed.at[rows], other.at[rows], feat_send.at[i], feat_recv.at[i], to_peer)

    own(0)
    feature(0).start()
    feature(1).start()
    own(1)

    mine_rows = pl.ds(pl.multiple_of(part * width, width), width)
    peer_rows = pl.ds(pl.multiple_of(peer * width, width), width)

    query_hot = (
        lax.broadcasted_iota(jnp.int32, (cap, tokens), 1) == query_col[...]
    ).astype(BF16)
    key_hot = (lax.broadcasted_iota(jnp.int32, (cap, tokens), 1) == key_col[...]).astype(BF16)
    inputs[0, :, mine_rows] = dot(query_hot, normed[...]).astype(BF16)
    inputs[1, :, mine_rows] = dot(key_hot, normed[...]).astype(BF16)
    load_qkv.wait()
    for j in range(3):
        share[j] = dot(normed[...], wide[j, mine_rows, :])
    def project(i):
        feature(i).wait_recv()
        rows = pl.ds(i * half, half)
        for j in range(3):
            value = share[j, rows, :] + dot(other[rows, :], wide[j, peer_rows, :])
            if j == 0:
                queries[rows, :] = value.astype(BF16)
            else:
                window[pl.ds(RADIUS + i * half, half), pl.ds((j - 1) * size, size)] = value.astype(
                    BF16
                )

    advance(0, 2)
    project(0)
    advance(0, 3)
    project(1)

    edge = pl.ds(RADIUS, RADIUS)
    last = pl.ds(tokens, RADIUS)
    halos = [
        remote(
            window.at[edge],
            window.at[pl.ds(tokens + RADIUS, RADIUS)],
            halo_send.at[0],
            halo_recv.at[0],
            {"seq": left},
        ),
        remote(
            window.at[last],
            window.at[pl.ds(0, RADIUS)],
            halo_send.at[1],
            halo_recv.at[1],
            {"seq": right},
        ),
    ]
    for halo in halos:
        halo.start()

    inputs[0, :, peer_rows] = dot(query_hot, other[...]).astype(BF16)
    inputs[1, :, peer_rows] = dot(key_hot, other[...]).astype(BF16)
    advance(0)
    gathered(0)
    slots = pl.ds(pl.multiple_of(me * cap, cap), cap)
    heavy_kv[slots, pl.ds(0, size)] = dot(inputs[1], pool[0]).astype(BF16)
    heavy_kv[slots, pl.ds(size, size)] = dot(inputs[1], pool[1]).astype(BF16)
    heavy_kv[slots, pl.ds(2 * size, BLOCK)] = (
        lax.broadcasted_iota(jnp.int32, (cap, BLOCK), 0) < key_count[...]
    ).astype(BF16)
    own(2)
    advance(1, 2)
    load_out.wait()
    blocks = tokens // BLOCK

    def outgoing(r):
        rows = pl.ds(pl.multiple_of(r * BLOCK, BLOCK), BLOCK)
        return remote(away.at[rows], arrived.at[rows], out_send.at[r], out_recv.at[r], to_peer)

    def block(r):
        rows = pl.ds(pl.multiple_of(r * BLOCK, BLOCK), BLOCK)
        reach = pl.ds(pl.multiple_of(r * BLOCK, BLOCK), BLOCK + 2 * RADIUS)
        shape = (2 * BLOCK, BLOCK + 2 * RADIUS)
        row = lax.broadcasted_iota(jnp.int32, shape, 0)
        row = jnp.where(row < BLOCK, row, row - BLOCK)
        column = lax.broadcasted_iota(jnp.int32, shape, 1)
        gap = column - row
        place = me * tokens + r * BLOCK - RADIUS + column
        allowed = (gap >= 0) & (gap <= 2 * RADIUS) & (place >= 0) & (place < count * tokens)
        for h in range(size // PAIR):
            lanes = pl.ds(h * PAIR, PAIR)
            context[rows, lanes] = attend(
                queries[rows, lanes],
                window[reach, lanes],
                window[reach, pl.ds(size + h * PAIR, PAIR)],
                allowed,
                scale,
            )
        away[rows, :] = dot(context[rows, :], narrow[:, peer_rows]).astype(BF16)
        outgoing(r).start()

    def inner(r, carry):
        block(r)
        return carry

    lax.fori_loop(1, blocks - 1, inner, 0)
    advance(1, 2)
    for halo in halos:
        halo.wait_recv()

    def outer(e, carry):
        block(e * (blocks - 1))
        return carry

    lax.fori_loop(0, 2, outer, 0)
    advance(1)
    advance(2, 2)
    pieces = width // size
    for j in range(pieces):
        columns = pl.ds(pl.multiple_of(part * width + j * size, BLOCK), size)
        share[j] = dot(context[...], narrow[:, columns])
    advance(2)
    gathered(1)
    heavy_q = dot(inputs[0], pool[2]).astype(BF16)
    logit = jnp.sum(
        inputs[0].astype(F32) * router[...].astype(F32), axis=1, keepdims=True
    )
    gate = 1.0 / (1.0 + jnp.exp(-logit))
    live_slot = lax.broadcasted_iota(jnp.int32, (cap, 1), 0) < query_count[...]
    gate = jnp.where(live_slot, gate, 0.0)
    gathered(2)
    first = (lax.broadcasted_iota(jnp.int32, (2 * cap, BLOCK), 1) == 0).astype(BF16)
    live = dot_nt(first, heavy_kv[:, pl.ds(2 * size, BLOCK)]) > 0.5
    heavy_context = jnp.concatenate(
        [
            attend(
                heavy_q[:, h * PAIR : (h + 1) * PAIR],
                heavy_kv[:, pl.ds(h * PAIR, PAIR)],
                heavy_kv[:, pl.ds(size + h * PAIR, PAIR)],
                live,
                scale,
            )
            for h in range(size // PAIR)
        ],
        axis=1,
    )
    rows_away[...] = dot_nt(heavy_context, pool[3, peer_rows, :]) * gate
    row_copy = remote(rows_away, rows_in, row_send.at[0], row_recv.at[0], to_peer)
    row_copy.start()
    rows_mine = dot_nt(heavy_context, pool[3, mine_rows, :]) * gate
    place_hot = (
        lax.broadcasted_iota(jnp.int32, (tokens, cap), 0) == query_row[...]
    ).astype(BF16)
    row_copy.wait_recv()
    routed = (rows_mine + rows_in[...]).astype(BF16)
    for r in [*range(1, blocks - 1), 0, blocks - 1]:
        outgoing(r).wait_recv()
        rows = pl.ds(r * BLOCK, BLOCK)
        for j in range(pieces):
            columns = pl.ds(j * size, size)
            added = dot(place_hot[r * BLOCK : (r + 1) * BLOCK], routed[:, j * size : (j + 1) * size])
            result[rows, columns] = (
                share[j, rows, :] + arrived[rows, columns].astype(F32) + added
            ).astype(BF16)

    for chunk in range(3):
        drain(chunk)
    for i in range(2):
        feature(i).wait_send()
        halos[i].wait_send()
    for r in range(blocks):
        outgoing(r).wait_send()
    row_copy.wait_send()


def shards(
    count,
    normed,
    router,
    light_qkv,
    light_out,
    heavy_qkv,
    heavy_out,
    query_slots,
    query_count,
    key_slots,
    key_count,
):
    tokens, width = normed.shape
    size = light_out.shape[0]
    model = router.shape[0]
    cap = query_slots.shape[1]
    levels = count // 4
    heavy = jnp.concatenate(
        [heavy_qkv[1:], heavy_qkv[:1], jnp.transpose(heavy_out)[None]], axis=0
    )
    vmem = pl.BlockSpec(memory_space=pltpu.VMEM)
    anywhere = pl.BlockSpec(memory_space=pl.ANY)
    blocks = tokens // BLOCK
    dma = pltpu.SemaphoreType.DMA
    return pl.pallas_call(
        functools.partial(kernel, count),
        out_shape=jax.ShapeDtypeStruct((tokens, width), BF16),
        in_specs=[vmem, vmem, anywhere, anywhere] + [vmem] * 6,
        out_specs=vmem,
        scratch_shapes=[
            pltpu.VMEM((tokens, width), BF16),
            pltpu.VMEM(light_qkv.shape, BF16),
            pltpu.VMEM(light_out.shape, BF16),
            pltpu.VMEM((4, model, size), BF16),
            pltpu.VMEM((3, tokens, size), F32),
            pltpu.VMEM((tokens, size), BF16),
            pltpu.VMEM((tokens + 2 * RADIUS, 2 * size), BF16),
            pltpu.VMEM((tokens, size), BF16),
            pltpu.VMEM((tokens, width), BF16),
            pltpu.VMEM((tokens, width), BF16),
            pltpu.VMEM((2, cap, model), BF16),
            pltpu.VMEM((count * cap, 2 * size + BLOCK), BF16),
            pltpu.VMEM((cap, width), F32),
            pltpu.VMEM((cap, width), F32),
            dma((2,)),
            dma((3, count)),
            dma((3, levels)),
            dma((3, levels)),
            dma((3, levels)),
            dma((3, 2 * levels)),
            dma((2,)),
            dma((2,)),
            dma((2,)),
            dma((2,)),
            dma((blocks,)),
            dma((blocks,)),
            dma((1,)),
            dma((1,)),
        ],
        compiler_params=pltpu.CompilerParams(
            collective_id=0, has_side_effects=True, vmem_limit_bytes=52 * 1024 * 1024
        ),
    )(
        normed,
        router[None],
        light_qkv,
        light_out,
        heavy,
        jnp.reshape(query_slots, (cap, 1)),
        query_slots,
        jnp.reshape(key_slots, (cap, 1)),
        query_count[None],
        key_count[None],
    )


def solution(mesh):
    in_specs = (
        P("seq", "mp"),
        P(),
        P(None, None, "mp"),
        P("mp", None),
        P(None, "seq", "mp"),
        P("mp", "seq"),
        P("seq", None),
        P("seq"),
        P("seq", None),
        P("seq"),
    )
    return jax.shard_map(
        functools.partial(shards, mesh.shape["seq"]),
        mesh=mesh,
        in_specs=in_specs,
        out_specs=P("seq", "mp"),
        check_vma=False,
    )
```

time: 229 us -> 88.5 us (0.39)
  Pallas kernels: 0 us -> 80.1 us
  blocking collectives: 76.3 us -> 0 us
  waiting for transfers between devices: 76.2 us -> 0 us
  matrix products: 34.9 us -> 0 us
  between operations: 15.3 us -> 1.34 us
  other arithmetic: 11.7 us -> 0.06 us
  local copies, waits for them, and re-layouts: 11.2 us -> 6.68 us
  starting transfers between devices: 2.87 us -> 0 us
    pallas_call x0 -> x1, Pallas kernels: none -> 80.1 us  [shards(): pl.pallas_call(functools.partial(kernel, count), out_shape=jax.ShapeDtype...]
    reduce_scatter x1 -> x0, waiting for transfers between devices: 51.9 us -> none  [shards(): lax.psum_scatter(combined, 'mp', scatter_dimension=1, tiled=True)]
    all_gather x2 -> x0, blocking collectives: 41.3 us -> none  [the longest x1 20.8 us: shards(): key_part = lax.all_gather(heavy_key, 'seq', axis=0, tiled=True)]
    unnamed x1 -> x0, blocking collectives: 34.9 us -> none
    dot_general x11 -> x0, matrix products: 26.4 us -> none  [the longest x1 5.29 us: shards(): jnp.einsum('td,cdh->cth', features, light_qkv[1:], preferred_element_type...]
    all_gather x3 -> x0, waiting for transfers between devices: 22.2 us -> none  [the longest x1 22.2 us: shards(): portion = lax.all_gather(heavy_qkv, 'seq', axis=1, tiled=True)]
    sub x1 -> x0, matrix products: 8.44 us -> none  [mix_heads(): weights = jnp.where(allowed[None], jnp.exp(scores - row_peak), 0.0)]
    gather x2 -> x0, local copies, waits for them, and re-layouts: 5.32 us -> none  [the longest x1 2.69 us: shards(): key_inputs = features[key_slots[0]]]
  transfers between devices with their start and end apart: 6 -> 0, of which waited for: 2 -> 0; matrix products, arithmetic and copies ran while one was open for 21% -> 0% of each run, Pallas kernels for 0% -> 0%
where the time goes in v2:
time: 88.5 us; the launch traced here: 88.2 us
  Pallas kernels  80.1 us (91%)
  local copies, waits for them, and re-layouts  6.68 us (8%)
  between operations  1.34 us (2%)
    pallas_call x1, Pallas kernels, shards(): pl.pallas_call(functools.partial(kernel, count), out_shape=jax.ShapeDtype...  80.1 us
    unnamed x4, local copies, waits for them, and re-layouts  2.63 us

profile of v2, /device:TPU:0, one launch (start us, length us, event | category | flops | bytes accessed | tf_op | source)
XLA Modules:
  0.0 88.2 jit_solution(18167520475779303014)
XLA Ops:
  1.3 0.7 broadcast_in_dim.12.router
  2.0 0.7 copy.13.key_col
  2.7 0.7 copy.12.query_col
  3.5 1.0 %copy.11 = bf16[512,128]{0,1:T(8,128)(2,1)S(1)} copy(bf16[512,128]{1,0:T(8,128)(2,1)} %param.15) | data formatting | bytes 262144 | tf_op args[5]
  4.5 0.9 %slice.7 = bf16[1,128,512]{2,1,0:T(8,128)(2,1)S(1)} slice(bf16[3,128,512]{2,1,0:T(8,128)(2,1)} %param.14), slice={[0:1], [0:128], [0:512]} | slice | bytes 262144 | tf_op jit(solution)/shard_map/slice | solution.py:441
  5.4 1.0 %slice.6 = bf16[2,128,512]{2,1,0:T(8,128)(2,1)S(1)} slice(bf16[3,128,512]{2,1,0:T(8,128)(2,1)} %param.14), slice={[1:3], [0:128], [0:512]} | slice | bytes 524288 | tf_op jit(solution)/shard_map/slice | solution.py:441
  6.4 0.1 pad_maximum_fusion.heavy
  6.4 0.0 copy-start
  6.5 0.6 copy-done
  7.1 80.1 %shard_map.100 = bf16[512,1024]{1,0:T(8,128)(2,1)S(1)} custom-call(bf16[512,1024]{1,0:T(8,128)(2,1)} %normed.1, bf16[1,2048]{1,0:T(2,128)(2,1)S(1)} %broadcast_in_dim.12.router, bf16[3,2048,512]{2,1,0:T(8,128)(2,1)} %light_qkv.1, bf16[512,2048]{1,0:T(8,128)(2,1)} %light_out.1, bf16[4,128,512]{2,1,0:T(8,128)(2,1)S(1)} %pad_maximum_fusion.heavy, ...), custom_call_target="tpu_custom_call" | custom-call | tf_op jit(solution)/shard_map/pallas_call | solution.py:447
  87.3 1.0 %copy.17 = bf16[512,1024]{1,0:T(8,128)(2,1)} copy(bf16[512,1024]{1,0:T(8,128)(2,1)S(1)} %shard_map.100) | data formatting | bytes 2097152
Async XLA Ops:
  6.4 0.7 copy-start

commit v3 on v2

--- a/solution.py
+++ b/solution.py
@@ -24,6 +24,10 @@
 
 def dot_nt(a, b):
     return lax.dot_general(a, b, NT, preferred_element_type=F32)
+
+
+def dot_tn(a, b):
+    return lax.dot_general(a, b, (((0,), (0,)), ((), ())), preferred_element_type=F32)
 
 
 def attend(q, k, v, allowed, scale):
@@ -44,10 +48,10 @@
     router,
     light_qkv,
     light_out,
-    heavy,
-    query_col,
+    heavy_qkv,
+    heavy_out,
     query_row,
-    key_col,
+    key_row,
     query_count,
     key_count,
     result,
@@ -82,8 +86,8 @@
 ):
     tokens, width = normed.shape
     size = narrow.shape[0]
-    depth = heavy.shape[1]
-    cap = key_col.shape[0]
+    depth = heavy_qkv.shape[1]
+    cap = key_row.shape[1]
     scale = HEAD_DIM ** (-0.5)
     me = lax.axis_index("seq")
     part = lax.axis_index("mp")
@@ -122,7 +126,12 @@
     load_qkv.start()
     load_out = pltpu.make_async_copy(light_out, narrow, load_sem.at[1])
     load_out.start()
-    pool[:, pl.ds(pl.multiple_of(me * depth, depth), depth), :] = heavy[...]
+    held = pl.ds(pl.multiple_of(me * depth, depth), depth)
+    for to, source in ((0, 1), (1, 2), (2, 0)):
+        pool[to, held, :] = heavy_qkv[source]
+    square = (depth, depth)
+    unit = lax.broadcasted_iota(jnp.int32, square, 0) == lax.broadcasted_iota(jnp.int32, square, 1)
+    pool[3, held, :] = dot_nt(unit.astype(BF16), heavy_out[...]).astype(BF16)
 
     pl.semaphore_wait(barrier, 5 + top.astype(jnp.int32) + bottom.astype(jnp.int32))
 
@@ -137,9 +146,10 @@
         )
 
     def view(chunk, s):
-        if chunk < 2:
+        if chunk != 2:
             rows = pl.ds(pl.multiple_of(s * depth, depth), depth)
-            return pool.at[pl.ds(2 * chunk, 2), rows, :]
+            first, many = {0: (0, 2), 1: (2, 1), 3: (3, 1)}[chunk]
+            return pool.at[pl.ds(first, many), rows, :]
         return heavy_kv.at[pl.ds(pl.multiple_of(s * cap, cap), cap), :]
 
     def hop(chunk, s, send, dest):
@@ -216,7 +226,7 @@
             yield functools.partial(across, chunk, d - 1)
         yield functools.partial(across, chunk, levels - 1)
 
-    pending = [list(events(chunk)) for chunk in range(3)]
+    pending = [list(events(chunk)) for chunk in range(4)]
 
     def advance(chunk, steps=None):
         steps = len(pending[chunk]) if steps is None else min(steps, len(pending[chunk]))
@@ -252,17 +262,14 @@
     own(0)
     feature(0).start()
     feature(1).start()
-    own(1)
-
     mine_rows = pl.ds(pl.multiple_of(part * width, width), width)
     peer_rows = pl.ds(pl.multiple_of(peer * width, width), width)
 
-    query_hot = (
-        lax.broadcasted_iota(jnp.int32, (cap, tokens), 1) == query_col[...]
-    ).astype(BF16)
-    key_hot = (lax.broadcasted_iota(jnp.int32, (cap, tokens), 1) == key_col[...]).astype(BF16)
-    inputs[0, :, mine_rows] = dot(query_hot, normed[...]).astype(BF16)
-    inputs[1, :, mine_rows] = dot(key_hot, normed[...]).astype(BF16)
+    tall = (tokens, cap)
+    query_hot = (lax.broadcasted_iota(jnp.int32, tall, 0) == query_row[...]).astype(BF16)
+    key_hot = (lax.broadcasted_iota(jnp.int32, tall, 0) == key_row[...]).astype(BF16)
+    inputs[0, :, mine_rows] = dot_tn(query_hot, normed[...]).astype(BF16)
+    inputs[1, :, mine_rows] = dot_tn(key_hot, normed[...]).astype(BF16)
     load_qkv.wait()
     for j in range(3):
         share[j] = dot(normed[...], wide[j, mine_rows, :])
@@ -279,8 +286,13 @@
                 )
 
     advance(0, 2)
+    own(1)
+    advance(0, 2)
     project(0)
-    advance(0, 3)
+    advance(0, 1)
+    own(3)
+    advance(0, 1)
+    advance(1, 2)
     project(1)
 
     edge = pl.ds(RADIUS, RADIUS)
@@ -304,9 +316,10 @@
     for halo in halos:
         halo.start()
 
-    inputs[0, :, peer_rows] = dot(query_hot, other[...]).astype(BF16)
-    inputs[1, :, peer_rows] = dot(key_hot, other[...]).astype(BF16)
+    inputs[0, :, peer_rows] = dot_tn(query_hot, other[...]).astype(BF16)
+    inputs[1, :, peer_rows] = dot_tn(key_hot, other[...]).astype(BF16)
     advance(0)
+    advance(1, 2)
     gathered(0)
     slots = pl.ds(pl.multiple_of(me * cap, cap), cap)
     heavy_kv[slots, pl.ds(0, size)] = dot(inputs[1], pool[0]).astype(BF16)
@@ -315,7 +328,8 @@
         lax.broadcasted_iota(jnp.int32, (cap, BLOCK), 0) < key_count[...]
     ).astype(BF16)
     own(2)
-    advance(1, 2)
+    advance(1)
+    advance(3, 2)
     load_out.wait()
     blocks = tokens // BLOCK
 
@@ -345,31 +359,24 @@
         away[rows, :] = dot(context[rows, :], narrow[:, peer_rows]).astype(BF16)
         outgoing(r).start()
 
-    def inner(r, carry):
+    for r in range(1, blocks - 1):
         block(r)
-        return carry
-
-    lax.fori_loop(1, blocks - 1, inner, 0)
-    advance(1, 2)
+        advance(2, 2)
+        advance(3, 2)
     for halo in halos:
         halo.wait_recv()
-
-    def outer(e, carry):
-        block(e * (blocks - 1))
-        return carry
-
-    lax.fori_loop(0, 2, outer, 0)
-    advance(1)
-    advance(2, 2)
+    block(0)
+    advance(2)
+    advance(3)
+    block(blocks - 1)
     pieces = width // size
     for j in range(pieces):
         columns = pl.ds(pl.multiple_of(part * width + j * size, BLOCK), size)
         share[j] = dot(context[...], narrow[:, columns])
-    advance(2)
     gathered(1)
     heavy_q = dot(inputs[0], pool[2]).astype(BF16)
     logit = jnp.sum(
-        inputs[0].astype(F32) * router[...].astype(F32), axis=1, keepdims=True
+        inputs[0].astype(F32) * router[...].astype(F32)[None, :], axis=1, keepdims=True
     )
     gate = 1.0 / (1.0 + jnp.exp(-logit))
     live_slot = lax.broadcasted_iota(jnp.int32, (cap, 1), 0) < query_count[...]
@@ -390,13 +397,11 @@
         ],
         axis=1,
     )
+    gathered(3)
     rows_away[...] = dot_nt(heavy_context, pool[3, peer_rows, :]) * gate
     row_copy = remote(rows_away, rows_in, row_send.at[0], row_recv.at[0], to_peer)
     row_copy.start()
     rows_mine = dot_nt(heavy_context, pool[3, mine_rows, :]) * gate
-    place_hot = (
-        lax.broadcasted_iota(jnp.int32, (tokens, cap), 0) == query_row[...]
-    ).astype(BF16)
     row_copy.wait_recv()
     routed = (rows_mine + rows_in[...]).astype(BF16)
     for r in [*range(1, blocks - 1), 0, blocks - 1]:
@@ -404,12 +409,12 @@
         rows = pl.ds(r * BLOCK, BLOCK)
         for j in range(pieces):
             columns = pl.ds(j * size, size)
-            added = dot(place_hot[r * BLOCK : (r + 1) * BLOCK], routed[:, j * size : (j + 1) * size])
+            added = dot(query_hot[r * BLOCK : (r + 1) * BLOCK], routed[:, j * size : (j + 1) * size])
             result[rows, columns] = (
                 share[j, rows, :] + arrived[rows, columns].astype(F32) + added
             ).astype(BF16)
 
-    for chunk in range(3):
+    for chunk in range(4):
         drain(chunk)
     for i in range(2):
         feature(i).wait_send()
@@ -437,9 +442,6 @@
     model = router.shape[0]
     cap = query_slots.shape[1]
     levels = count // 4
-    heavy = jnp.concatenate(
-        [heavy_qkv[1:], heavy_qkv[:1], jnp.transpose(heavy_out)[None]], axis=0
-    )
     vmem = pl.BlockSpec(memory_space=pltpu.VMEM)
     anywhere = pl.BlockSpec(memory_space=pl.ANY)
     blocks = tokens // BLOCK
@@ -465,11 +467,11 @@
             pltpu.VMEM((cap, width), F32),
             pltpu.VMEM((cap, width), F32),
             dma((2,)),
-            dma((3, count)),
-            dma((3, levels)),
-            dma((3, levels)),
-            dma((3, levels)),
-            dma((3, 2 * levels)),
+            dma((4, count)),
+            dma((4, levels)),
+            dma((4, levels)),
+            dma((4, levels)),
+            dma((4, 2 * levels)),
             dma((2,)),
             dma((2,)),
             dma((2,)),
@@ -484,13 +486,13 @@
         ),
     )(
         normed,
-        router[None],
+        router,
         light_qkv,
         light_out,
-        heavy,
-        jnp.reshape(query_slots, (cap, 1)),
+        heavy_qkv,
+        heavy_out,
         query_slots,
-        jnp.reshape(key_slots, (cap, 1)),
+        key_slots,
         query_count[None],
         key_count[None],
     )

time: 88.5 us -> 86.9 us (0.982)
  local copies, waits for them, and re-layouts: 6.68 us -> 4.86 us
    unnamed x4 -> x11, local copies, waits for them, and re-layouts: 2.63 us -> 4.86 us
    slice x2 -> x0, local copies, waits for them, and re-layouts: 1.89 us -> none  [the longest x1 0.97 us: shards(): heavy_qkv[1:]]
    reshape x2 -> x0, local copies, waits for them, and re-layouts: 1.47 us -> none  [the longest x1 0.74 us: shards(): jnp.reshape(key_slots, (cap, 1))]
where the time goes in v3:
time: 86.9 us; the launch traced here: 86.7 us
  Pallas kernels  80.5 us (93%)
  local copies, waits for them, and re-layouts  4.86 us (6%)
  between operations  1.32 us (2%)
    pallas_call x1, Pallas kernels, shards(): pl.pallas_call(functools.partial(kernel, count), out_shape=jax.ShapeDtype...  80.5 us
    unnamed x11, local copies, waits for them, and re-layouts  4.86 us

profile of v3, /device:TPU:0, one launch (start us, length us, event | category | flops | bytes accessed | tf_op | source)
XLA Modules:
  0.0 86.7 jit_solution(15080170430181594776)
XLA Ops:
  1.3 0.0 copy-start
  1.3 1.0 %copy-done = bf16[3,128,512]{2,1,0:T(8,128)(2,1)S(1)} copy-done((bf16[3,128,512]{2,1,0:T(8,128)(2,1)S(1)}, bf16[3,128,512]{2,1,0:T(8,128)(2,1)}, u32[]{:S(2)}) %copy-start) | copy-done | bytes 393240
  2.3 0.0 copy-start.1
  2.3 0.9 %copy-done.1 = bf16[512,128]{1,0:T(8,128)(2,1)S(1)} copy-done((bf16[512,128]{1,0:T(8,128)(2,1)S(1)}, bf16[512,128]{1,0:T(8,128)(2,1)}, u32[]{:S(2)}) %copy-start.1) | copy-done | bytes 131096
  3.2 0.0 copy-start.2
  3.2 0.7 copy-done.2
  3.9 0.0 copy-start.3
  3.9 0.7 copy-done.3
  4.5 0.0 copy-start.4
  4.5 0.7 copy-done.4
  5.2 80.5 %shard_map.100 = bf16[512,1024]{1,0:T(8,128)(2,1)S(1)} custom-call(bf16[512,1024]{1,0:T(8,128)(2,1)} %normed.1, bf16[2048]{0:T(1024)(128)(2,1)S(1)} %copy-done.2, bf16[3,2048,512]{2,1,0:T(8,128)(2,1)} %light_qkv.1, bf16[512,2048]{1,0:T(8,128)(2,1)} %light_out.1, bf16[3,128,512]{2,1,0:T(8,128)(2,1)S(1)} %copy-done, bf16[512,128]{1,0:T(8,128)(2,1)S(1)} %copy-done.1, ...), custom_call_target="tpu_custom_call" | custom-call | tf_op jit(solution)/shard_map/pallas_call | solution.py:449
  85.7 1.0 %copy.14 = bf16[512,1024]{1,0:T(8,128)(2,1)} copy(bf16[512,1024]{1,0:T(8,128)(2,1)S(1)} %shard_map.100) | data formatting | bytes 2097152
Async XLA Ops:
  1.3 1.0 %copy-start = (bf16[3,128,512]{2,1,0:T(8,128)(2,1)S(1)}, bf16[3,128,512]{2,1,0:T(8,128)(2,1)}, u32[]{:S(2)}) copy-start(bf16[3,128,512]{2,1,0:T(8,128)(2,1)} %heavy_qkv.1) | copy-start | bytes 1179652
  2.3 0.9 %copy-start.1 = (bf16[512,128]{1,0:T(8,128)(2,1)S(1)}, bf16[512,128]{1,0:T(8,128)(2,1)}, u32[]{:S(2)}) copy-start(bf16[512,128]{1,0:T(8,128)(2,1)} %heavy_out.1) | copy-start | bytes 393220
  3.2 0.7 copy-start.2
  3.9 0.7 copy-start.3
  4.5 0.7 copy-start.4
